TPU v7x, 32 devices: a whole 2x2x4 slice. The times are simulated.
32 devices in a mesh: groups: 2 (over y), row: 4 (over z), col: 4 (over x, core).
Axes of the slice: x: 2, y: 2, z: 4, core: 2. Of those that a mesh axis runs over, the one named last changes fastest.
Arguments:
- features: bfloat16 [8, 2048, 256], P(('groups', 'row'), 'col'), parts along dimension 0, may hold values from -6 to 6
- tile_values: bfloat16 [8, 4, 1024, 4096], P(('groups', 'row'), 'col'), parts along dimension 0, may hold values from -0.125 to 0.125
- tile_rows: int32 [8, 4, 1024], P(('groups', 'row'), 'col'), parts along dimension 0, may hold values from 0 to 31
- tile_cols: int32 [8, 4, 1024], P(('groups', 'row'), 'col'), parts along dimension 0, may hold values from 0 to 31
- counts: int32 [8, 4], P(('groups', 'row'), 'col'), parts along dimension 0, may hold values from 128 to 1024, as said below
- weight: bfloat16 [256, 256], replicated, may hold values from -0.375 to 0.375
- bias: float32 [256], replicated, may hold values from -3 to 3
Outputs:
- layer_out: bfloat16 [8, 2048, 256], P(('groups', 'col'), 'row'), parts along dimension 0
There are 2 independent parts, one for each index of `groups`. A program takes and returns all parts, laid end to end along the dimension named above; an argument that names none is the same for every part. Nothing has to cross between parts.
Inputs may be any that keep to these rules, and one draw needn't show every extreme that they name: Slots at or past counts[r, c] hold values that are to be ignored; coordinate pairs may repeat within a cell, and repeated tiles add. In every draw one grid cell has exactly 1024 live slots.
All inputs are finite; a program needn't handle non-finite values.
Results may differ from a plain program's by a relative error of at most 0.0046.
Values may be sent and summed in bfloat16 or wider, within the bound.
A program may use at most 128 MiB of HBM per device.

v0:
```python
import jax
import jax.numpy as jnp
from jax import lax
from jax.sharding import PartitionSpec as P

TILE = 64


def on_device(features, tile_values, tile_rows, tile_cols, counts, weight, bias):
    piece_rows = features.shape[1]
    feat_width = features.shape[2]
    gathered = lax.all_gather(features, "col", axis=1, tiled=True)
    source = gathered.reshape(-1, TILE, feat_width)
    slot_count = tile_values.shape[2]
    block_size = min(128, slot_count)
    out_tiles = lax.axis_size("row") * piece_rows // TILE
    values = tile_values.reshape(slot_count, TILE, TILE)
    tile_row = tile_rows.reshape(slot_count)
    tile_col = tile_cols.reshape(slot_count)
    live_count = counts.reshape(())
    tile_ids = jnp.arange(out_tiles, dtype=jnp.int32)

    def block_step(block_index, running):
        first_slot = block_index * block_size
        tile_block = lax.dynamic_slice_in_dim(values, first_slot, block_size, 0)
        target_rows = lax.dynamic_slice_in_dim(tile_row, first_slot, block_size, 0)
        source_cols = lax.dynamic_slice_in_dim(tile_col, first_slot, block_size, 0)
        inputs = source[source_cols]
        products = jnp.einsum(
            "bij,bjf->bif", tile_block, inputs, preferred_element_type=jnp.float32
        )
        is_live = first_slot + jnp.arange(block_size, dtype=jnp.int32) < live_count
        target = jnp.where(is_live, target_rows, out_tiles)
        selector = (tile_ids[:, None] == target[None, :]).astype(jnp.float32)
        flat_products = products.reshape(block_size, TILE * feat_width)
        added = jnp.dot(
            selector,
            flat_products,
            precision=lax.Precision.HIGHEST,
            preferred_element_type=jnp.float32,
        )
        return running + added

    running = jnp.zeros((out_tiles, TILE * feat_width), jnp.float32)
    block_count = slot_count // block_size
    running = lax.fori_loop(0, block_count, block_step, running)
    partial_value = running.reshape(-1, feat_width)
    own_rows = lax.psum_scatter(partial_value, "row", scatter_dimension=0, tiled=True)
    hidden = own_rows.astype(jnp.bfloat16)
    mixed = jnp.dot(hidden, weight, preferred_element_type=jnp.float32) + bias
    return jnp.maximum(mixed, 0.0).astype(jnp.bfloat16).reshape(1, piece_rows, feat_width)


def solution(mesh):
    in_specs = (
        P(("groups", "row"), "col", None),
        P(("groups", "row"), "col", None, None),
        P(("groups", "row"), "col", None),
        P(("groups", "row"), "col", None),
        P(("groups", "row"), "col"),
        P(),
        P(),
    )
    out_specs = P(("groups", "col"), "row", None)
    return jax.shard_map(
        on_device, mesh=mesh, in_specs=in_specs, out_specs=out_specs, check_vma=False
    )
```

profile of v0, /device:TPU:0, one launch (start us, length us, event | category | flops | bytes accessed | tf_op | source)
XLA Modules:
  0.0 323.3 jit_solution(16852734257840605443)
XLA Ops:
  7.3 12.0 %copy.8 = bf16[1,1,1024,4096]{2,3,1,0:T(8,128)(2,1)} copy(bf16[1,1,1024,4096]{3,2,1,0:T(8,128)(2,1)} %param.10) | data formatting | bytes 16777216 | tf_op args[1]
  19.4 9.0 %all-gather.2.cloned.1.call-done = bf16[1,2048,256]{2,1,0:T(8,128)(2,1)} async-done(((bf16[1,512,256]{2,1,0:T(8,128)(2,1)}), bf16[1,2048,256]{2,1,0:T(8,128)(2,1)}) %all-gather.2.cloned.1.call-update) | async-done | bytes 1048592 | tf_op jit(solution)/shard_map/all_gather | solution.py:12
  28.4 239.3 %while.14 = (s32[]{:T(128)}, f32[32,16384]{1,0:T(8,128)}, s32[]{:T(128)}, s32[1024]{0:T(1024)}, bf16[1024,64,64]{0,2,1:T(8,128)(2,1)}, /*index=5*/s32[1024]{0:T(...) while((s32[]{:T(128)}, f32[32,16384]{1,0:T(8,128)}, ...), condition=%wide.region_1.2_spmd.clone, body=%wide.region_0.1_spmd.clone.sunk | while | flops 1074796288 | bytes 72359656 | solution.py:46
  28.4 1.4 compare_select_fusion.3
  29.8 4.0 %gather_fusion = bf16[128,64,256]{2,1,0:T(8,128)(2,1)} fusion(bf16[32,64,256]{2,1,0:T(8,128)(2,1)} %get-tuple-element.269, s32[1024]{0:T(1024)S(1)} %pad_clamp_fusion.2), kind=kCustom, calls=%fused_computation.clone.clone.1 | custom fusion | bytes 8389120 | tf_op jit(solution)/shard_map/while/body/eval_jaxpr/gather | solution.py:28
  35.1 3.0 copy.14
  38.1 3.4 %fusion.19 = f32[128,64,256]{2,1,0:T(8,128)S(1)} fusion(bf16[128,64,64]{2,1,0:T(8,128)(2,1)S(1)} %copy.14, bf16[128,64,256]{2,1,0:T(8,128)(2,1)} %gather_fusion), kind=kOutput, calls=%fused_computation.14.clone.1 | convolution fusion | flops 268435456 | bytes 13631488 | tf_op jit(solution)/shard_map/while/body/eval_jaxpr/bij,bjf->bif/dot_general | solution.py:29
  41.5 9.7 %copy.15 = f32[16,8,64,256]{3,1,2,0:T(8,128)} copy(f32[16,8,64,256]{3,2,1,0:T(8,128)S(1)} %bitcast.24) | data formatting | bytes 16777216 | tf_op jit(solution)/shard_map/while
  51.3 5.6 %convolution_add_fusion.3 = f32[32,16384]{1,0:T(8,128)S(1)} fusion(f32[128,16384]{1,0:T(8,128)} %bitcast.23, f32[32,16384]{1,0:T(8,128)S(1)} %copy-done.1, pred[]{:T(512)S(6)} %compare.3, s32[128]{0:T(128)S(1)} %get-tuple-element.240), kind=kOutput, calls=%fused_computation.2.clone.1 | convolution fusion | flops 806359040 | bytes 12583425 | tf_op jit(solution)/shard_map/while/body/eval_jaxpr/dot_general | solution.py:36
  59.7 4.0 %gather_fusion = bf16[128,64,256]{2,1,0:T(8,128)(2,1)} fusion(bf16[32,64,256]{2,1,0:T(8,128)(2,1)} %get-tuple-element.269, s32[1024]{0:T(1024)S(1)} %pad_clamp_fusion.2), kind=kCustom, calls=%fused_computation.clone.clone.1 | custom fusion | bytes 8389120 | tf_op jit(solution)/shard_map/while/body/eval_jaxpr/gather | solution.py:28
  65.0 3.0 copy.14
  68.0 3.4 %fusion.19 = f32[128,64,256]{2,1,0:T(8,128)S(1)} fusion(bf16[128,64,64]{2,1,0:T(8,128)(2,1)S(1)} %copy.14, bf16[128,64,256]{2,1,0:T(8,128)(2,1)} %gather_fusion), kind=kOutput, calls=%fused_computation.14.clone.1 | convolution fusion | flops 268435456 | bytes 13631488 | tf_op jit(solution)/shard_map/while/body/eval_jaxpr/bij,bjf->bif/dot_general | solution.py:29
  71.5 9.7 %copy.15 = f32[16,8,64,256]{3,1,2,0:T(8,128)} copy(f32[16,8,64,256]{3,2,1,0:T(8,128)S(1)} %bitcast.24) | data formatting | bytes 16777216 | tf_op jit(solution)/shard_map/while
  81.2 5.6 %convolution_add_fusion.3 = f32[32,16384]{1,0:T(8,128)S(1)} fusion(f32[128,16384]{1,0:T(8,128)} %bitcast.23, f32[32,16384]{1,0:T(8,128)S(1)} %copy-done.1, pred[]{:T(512)S(6)} %compare.3, s32[128]{0:T(128)S(1)} %get-tuple-element.240), kind=kOutput, calls=%fused_computation.2.clone.1 | convolution fusion | flops 806359040 | bytes 12583425 | tf_op jit(solution)/shard_map/while/body/eval_jaxpr/dot_general | solution.py:36
  88.2 1.4 compare_select_fusion.3
  89.6 4.0 %gather_fusion = bf16[128,64,256]{2,1,0:T(8,128)(2,1)} fusion(bf16[32,64,256]{2,1,0:T(8,128)(2,1)} %get-tuple-element.269, s32[1024]{0:T(1024)S(1)} %pad_clamp_fusion.2), kind=kCustom, calls=%fused_computation.clone.clone.1 | custom fusion | bytes 8389120 | tf_op jit(solution)/shard_map/while/body/eval_jaxpr/gather | solution.py:28
  94.9 3.0 copy.14
  97.9 3.4 %fusion.19 = f32[128,64,256]{2,1,0:T(8,128)S(1)} fusion(bf16[128,64,64]{2,1,0:T(8,128)(2,1)S(1)} %copy.14, bf16[128,64,256]{2,1,0:T(8,128)(2,1)} %gather_fusion), kind=kOutput, calls=%fused_computation.14.clone.1 | convolution fusion | flops 268435456 | bytes 13631488 | tf_op jit(solution)/shard_map/while/body/eval_jaxpr/bij,bjf->bif/dot_general | solution.py:29
  101.4 9.7 %copy.15 = f32[16,8,64,256]{3,1,2,0:T(8,128)} copy(f32[16,8,64,256]{3,2,1,0:T(8,128)S(1)} %bitcast.24) | data formatting | bytes 16777216 | tf_op jit(solution)/shard_map/while
  111.1 5.6 %convolution_add_fusion.3 = f32[32,16384]{1,0:T(8,128)S(1)} fusion(f32[128,16384]{1,0:T(8,128)} %bitcast.23, f32[32,16384]{1,0:T(8,128)S(1)} %copy-done.1, pred[]{:T(512)S(6)} %compare.3, s32[128]{0:T(128)S(1)} %get-tuple-element.240), kind=kOutput, calls=%fused_computation.2.clone.1 | convolution fusion | flops 806359040 | bytes 12583425 | tf_op jit(solution)/shard_map/while/body/eval_jaxpr/dot_general | solution.py:36
  119.5 4.0 %gather_fusion = bf16[128,64,256]{2,1,0:T(8,128)(2,1)} fusion(bf16[32,64,256]{2,1,0:T(8,128)(2,1)} %get-tuple-element.269, s32[1024]{0:T(1024)S(1)} %pad_clamp_fusion.2), kind=kCustom, calls=%fused_computation.clone.clone.1 | custom fusion | bytes 8389120 | tf_op jit(solution)/shard_map/while/body/eval_jaxpr/gather | solution.py:28
  124.8 3.0 copy.14
  127.8 3.4 %fusion.19 = f32[128,64,256]{2,1,0:T(8,128)S(1)} fusion(bf16[128,64,64]{2,1,0:T(8,128)(2,1)S(1)} %copy.14, bf16[128,64,256]{2,1,0:T(8,128)(2,1)} %gather_fusion), kind=kOutput, calls=%fused_computation.14.clone.1 | convolution fusion | flops 268435456 | bytes 13631488 | tf_op jit(solution)/shard_map/while/body/eval_jaxpr/bij,bjf->bif/dot_general | solution.py:29
  131.3 9.7 %copy.15 = f32[16,8,64,256]{3,1,2,0:T(8,128)} copy(f32[16,8,64,256]{3,2,1,0:T(8,128)S(1)} %bitcast.24) | data formatting | bytes 16777216 | tf_op jit(solution)/shard_map/while
  141.0 5.6 %convolution_add_fusion.3 = f32[32,16384]{1,0:T(8,128)S(1)} fusion(f32[128,16384]{1,0:T(8,128)} %bitcast.23, f32[32,16384]{1,0:T(8,128)S(1)} %copy-done.1, pred[]{:T(512)S(6)} %compare.3, s32[128]{0:T(128)S(1)} %get-tuple-element.240), kind=kOutput, calls=%fused_computation.2.clone.1 | convolution fusion | flops 806359040 | bytes 12583425 | tf_op jit(solution)/shard_map/while/body/eval_jaxpr/dot_general | solution.py:36
  149.4 4.0 %gather_fusion = bf16[128,64,256]{2,1,0:T(8,128)(2,1)} fusion(bf16[32,64,256]{2,1,0:T(8,128)(2,1)} %get-tuple-element.269, s32[1024]{0:T(1024)S(1)} %pad_clamp_fusion.2), kind=kCustom, calls=%fused_computation.clone.clone.1 | custom fusion | bytes 8389120 | tf_op jit(solution)/shard_map/while/body/eval_jaxpr/gather | solution.py:28
  154.7 3.0 copy.14
  157.7 3.4 %fusion.19 = f32[128,64,256]{2,1,0:T(8,128)S(1)} fusion(bf16[128,64,64]{2,1,0:T(8,128)(2,1)S(1)} %copy.14, bf16[128,64,256]{2,1,0:T(8,128)(2,1)} %gather_fusion), kind=kOutput, calls=%fused_computation.14.clone.1 | convolution fusion | flops 268435456 | bytes 13631488 | tf_op jit(solution)/shard_map/while/body/eval_jaxpr/bij,bjf->bif/dot_general | solution.py:29
  161.2 9.7 %copy.15 = f32[16,8,64,256]{3,1,2,0:T(8,128)} copy(f32[16,8,64,256]{3,2,1,0:T(8,128)S(1)} %bitcast.24) | data formatting | bytes 16777216 | tf_op jit(solution)/shard_map/while
  170.9 5.6 %convolution_add_fusion.3 = f32[32,16384]{1,0:T(8,128)S(1)} fusion(f32[128,16384]{1,0:T(8,128)} %bitcast.23, f32[32,16384]{1,0:T(8,128)S(1)} %copy-done.1, pred[]{:T(512)S(6)} %compare.3, s32[128]{0:T(128)S(1)} %get-tuple-element.240), kind=kOutput, calls=%fused_computation.2.clone.1 | convolution fusion | flops 806359040 | bytes 12583425 | tf_op jit(solution)/shard_map/while/body/eval_jaxpr/dot_general | solution.py:36
  179.3 4.0 %gather_fusion = bf16[128,64,256]{2,1,0:T(8,128)(2,1)} fusion(bf16[32,64,256]{2,1,0:T(8,128)(2,1)} %get-tuple-element.269, s32[1024]{0:T(1024)S(1)} %pad_clamp_fusion.2), kind=kCustom, calls=%fused_computation.clone.clone.1 | custom fusion | bytes 8389120 | tf_op jit(solution)/shard_map/while/body/eval_jaxpr/gather | solution.py:28
  184.7 3.0 copy.14
  187.7 3.4 %fusion.19 = f32[128,64,256]{2,1,0:T(8,128)S(1)} fusion(bf16[128,64,64]{2,1,0:T(8,128)(2,1)S(1)} %copy.14, bf16[128,64,256]{2,1,0:T(8,128)(2,1)} %gather_fusion), kind=kOutput, calls=%fused_computation.14.clone.1 | convolution fusion | flops 268435456 | bytes 13631488 | tf_op jit(solution)/shard_map/while/body/eval_jaxpr/bij,bjf->bif/dot_general | solution.py:29
  191.1 9.7 %copy.15 = f32[16,8,64,256]{3,1,2,0:T(8,128)} copy(f32[16,8,64,256]{3,2,1,0:T(8,128)S(1)} %bitcast.24) | data formatting | bytes 16777216 | tf_op jit(solution)/shard_map/while
  200.8 5.6 %convolution_add_fusion.3 = f32[32,16384]{1,0:T(8,128)S(1)} fusion(f32[128,16384]{1,0:T(8,128)} %bitcast.23, f32[32,16384]{1,0:T(8,128)S(1)} %copy-done.1, pred[]{:T(512)S(6)} %compare.3, s32[128]{0:T(128)S(1)} %get-tuple-element.240), kind=kOutput, calls=%fused_computation.2.clone.1 | convolution fusion | flops 806359040 | bytes 12583425 | tf_op jit(solution)/shard_map/while/body/eval_jaxpr/dot_general | solution.py:36
  209.3 4.0 %gather_fusion = bf16[128,64,256]{2,1,0:T(8,128)(2,1)} fusion(bf16[32,64,256]{2,1,0:T(8,128)(2,1)} %get-tuple-element.269, s32[1024]{0:T(1024)S(1)} %pad_clamp_fusion.2), kind=kCustom, calls=%fused_computation.clone.clone.1 | custom fusion | bytes 8389120 | tf_op jit(solution)/shard_map/while/body/eval_jaxpr/gather | solution.py:28
  214.6 3.0 copy.14
  217.6 3.4 %fusion.19 = f32[128,64,256]{2,1,0:T(8,128)S(1)} fusion(bf16[128,64,64]{2,1,0:T(8,128)(2,1)S(1)} %copy.14, bf16[128,64,256]{2,1,0:T(8,128)(2,1)} %gather_fusion), kind=kOutput, calls=%fused_computation.14.clone.1 | convolution fusion | flops 268435456 | bytes 13631488 | tf_op jit(solution)/shard_map/while/body/eval_jaxpr/bij,bjf->bif/dot_general | solution.py:29
  221.0 9.7 %copy.15 = f32[16,8,64,256]{3,1,2,0:T(8,128)} copy(f32[16,8,64,256]{3,2,1,0:T(8,128)S(1)} %bitcast.24) | data formatting | bytes 16777216 | tf_op jit(solution)/shard_map/while
  230.7 5.6 %convolution_add_fusion.3 = f32[32,16384]{1,0:T(8,128)S(1)} fusion(f32[128,16384]{1,0:T(8,128)} %bitcast.23, f32[32,16384]{1,0:T(8,128)S(1)} %copy-done.1, pred[]{:T(512)S(6)} %compare.3, s32[128]{0:T(128)S(1)} %get-tuple-element.240), kind=kOutput, calls=%fused_computation.2.clone.1 | convolution fusion | flops 806359040 | bytes 12583425 | tf_op jit(solution)/shard_map/while/body/eval_jaxpr/dot_general | solution.py:36
  239.2 4.0 %gather_fusion = bf16[128,64,256]{2,1,0:T(8,128)(2,1)} fusion(bf16[32,64,256]{2,1,0:T(8,128)(2,1)} %get-tuple-element.269, s32[1024]{0:T(1024)S(1)} %pad_clamp_fusion.2), kind=kCustom, calls=%fused_computation.clone.clone.1 | custom fusion | bytes 8389120 | tf_op jit(solution)/shard_map/while/body/eval_jaxpr/gather | solution.py:28
  244.5 3.0 copy.14
  247.5 3.4 %fusion.19 = f32[128,64,256]{2,1,0:T(8,128)S(1)} fusion(bf16[128,64,64]{2,1,0:T(8,128)(2,1)S(1)} %copy.14, bf16[128,64,256]{2,1,0:T(8,128)(2,1)} %gather_fusion), kind=kOutput, calls=%fused_computation.14.clone.1 | convolution fusion | flops 268435456 | bytes 13631488 | tf_op jit(solution)/shard_map/while/body/eval_jaxpr/bij,bjf->bif/dot_general | solution.py:29
  250.9 9.7 %copy.15 = f32[16,8,64,256]{3,1,2,0:T(8,128)} copy(f32[16,8,64,256]{3,2,1,0:T(8,128)S(1)} %bitcast.24) | data formatting | bytes 16777216 | tf_op jit(solution)/shard_map/while
  260.6 5.6 %convolution_add_fusion.3 = f32[32,16384]{1,0:T(8,128)S(1)} fusion(f32[128,16384]{1,0:T(8,128)} %bitcast.23, f32[32,16384]{1,0:T(8,128)S(1)} %copy-done.1, pred[]{:T(512)S(6)} %compare.3, s32[128]{0:T(128)S(1)} %get-tuple-element.240), kind=kOutput, calls=%fused_computation.2.clone.1 | convolution fusion | flops 806359040 | bytes 12583425 | tf_op jit(solution)/shard_map/while/body/eval_jaxpr/dot_general | solution.py:36
  267.6 2.7 reshape.36
  270.4 44.0 %reduce-scatter.2.cloned.1.call-done = f32[512,256]{1,0:T(8,128)} async-done(((f32[2048,256]{1,0:T(8,128)}), f32[512,256]{1,0:T(8,128)}) %reduce-scatter.2.cloned.1.call-update) | async-done | bytes 524304 | tf_op jit(solution)/shard_map/reduce_scatter | solution.py:48
  314.4 2.0 fusion.5
  (63 shorter events, 30.4 us)
Async XLA Ops:
  6.5 307.9 %copy-start = (bf16[256,256]{1,0:T(8,128)(2,1)S(1)}, bf16[256,256]{1,0:T(8,128)(2,1)}, u32[]{:S(2)}) copy-start(bf16[256,256]{1,0:T(8,128)(2,1)} %param.14) | copy-start | bytes 393220
  6.5 21.8 %all-gather.2.cloned.1.call-start = ((), (), s32[]{:S(2)}) async-start(), calls=%async_computation.1 | async-start | bytes 1310720 | tf_op jit(solution)/shard_map/all_gather | solution.py:12
  7.3 307.2 %reduce-scatter.2.cloned.1.call-start = ((), (), s32[]{:S(2)}) async-start(), calls=%async_computation.2 | async-start | bytes 2621440 | tf_op jit(solution)/shard_map/reduce_scatter | solution.py:48
  41.5 9.7 %copy-start.1 = (f32[32,16384]{1,0:T(8,128)S(1)}, f32[32,16384]{1,0:T(8,128)}, u32[]{:S(2)}) copy-start(f32[32,16384]{1,0:T(8,128)} %get-tuple-element.253) | copy-start | bytes 6291460 | tf_op jit(solution)/shard_map/while
  56.9 1.3 copy-start.2
  71.4 9.7 %copy-start.1 = (f32[32,16384]{1,0:T(8,128)S(1)}, f32[32,16384]{1,0:T(8,128)}, u32[]{:S(2)}) copy-start(f32[32,16384]{1,0:T(8,128)} %get-tuple-element.253) | copy-start | bytes 6291460 | tf_op jit(solution)/shard_map/while
  86.8 1.3 copy-start.2
  101.4 9.7 %copy-start.1 = (f32[32,16384]{1,0:T(8,128)S(1)}, f32[32,16384]{1,0:T(8,128)}, u32[]{:S(2)}) copy-start(f32[32,16384]{1,0:T(8,128)} %get-tuple-element.253) | copy-start | bytes 6291460 | tf_op jit(solution)/shard_map/while
  116.8 1.3 copy-start.2
  131.3 9.7 %copy-start.1 = (f32[32,16384]{1,0:T(8,128)S(1)}, f32[32,16384]{1,0:T(8,128)}, u32[]{:S(2)}) copy-start(f32[32,16384]{1,0:T(8,128)} %get-tuple-element.253) | copy-start | bytes 6291460 | tf_op jit(solution)/shard_map/while
  146.7 1.3 copy-start.2
  161.2 9.7 %copy-start.1 = (f32[32,16384]{1,0:T(8,128)S(1)}, f32[32,16384]{1,0:T(8,128)}, u32[]{:S(2)}) copy-start(f32[32,16384]{1,0:T(8,128)} %get-tuple-element.253) | copy-start | bytes 6291460 | tf_op jit(solution)/shard_map/while
  176.6 1.3 copy-start.2
  191.1 9.7 %copy-start.1 = (f32[32,16384]{1,0:T(8,128)S(1)}, f32[32,16384]{1,0:T(8,128)}, u32[]{:S(2)}) copy-start(f32[32,16384]{1,0:T(8,128)} %get-tuple-element.253) | copy-start | bytes 6291460 | tf_op jit(solution)/shard_map/while
  206.5 1.3 copy-start.2
  221.0 9.7 %copy-start.1 = (f32[32,16384]{1,0:T(8,128)S(1)}, f32[32,16384]{1,0:T(8,128)}, u32[]{:S(2)}) copy-start(f32[32,16384]{1,0:T(8,128)} %get-tuple-element.253) | copy-start | bytes 6291460 | tf_op jit(solution)/shard_map/while
  236.4 1.3 copy-start.2
  250.9 9.7 %copy-start.1 = (f32[32,16384]{1,0:T(8,128)S(1)}, f32[32,16384]{1,0:T(8,128)}, u32[]{:S(2)}) copy-start(f32[32,16384]{1,0:T(8,128)} %get-tuple-element.253) | copy-start | bytes 6291460 | tf_op jit(solution)/shard_map/while
  266.3 1.3 copy-start.2
  267.6 46.8 %copy-start.3 = (f32[256]{0:T(256)S(1)}, f32[256]{0:T(256)}, u32[]{:S(2)}) copy-start(f32[256]{0:T(256)} %param.15) | copy-start | bytes 3076
Sparse Core Ops, SparseCore 0:
  8.9 19.4 all-gather.1
  270.5 43.8 reduce-scatter.1
where the time goes:
time: 325 us; the launch traced here: 323 us
  local copies, waits for them, and re-layouts  170 us (52%)
  matrix products  74.5 us (23%)
  waiting for transfers between devices  53.8 us (17%)
  between operations  13.4 us (4%)
  other arithmetic  11.4 us (4%)
    while x40, local copies, waits for them, and re-layouts  88.5 us
    dot_general x8, matrix products, block_step(): jnp.dot(selector, flat_products, precision=lax.Precision.HIGHEST, preferr...  45.2 us
    reduce_scatter x1, waiting for transfers between devices, on_device(): lax.psum_scatter(partial_value, 'row', scatter_dimension=0, tiled=True)  44 us
    dynamic_slice x16, local copies, waits for them, and re-layouts, block_step(): tile_block = lax.dynamic_slice_in_dim(values, first_slot, block_size, 0)  34.2 us
    gather x8, local copies, waits for them, and re-layouts, block_step(): inputs = source[source_cols]  32.1 us
    dot_general x8, matrix products, block_step(): jnp.einsum('bij,bjf->bif', tile_block, inputs, preferred_element_type=jnp...  27.4 us
    unnamed x5, local copies, waits for them, and re-layouts  12 us
    select_n x8, other arithmetic, block_step(): inputs = source[source_cols]  11.4 us
  transfers between devices with their start and end apart: 2, of which 2 were waited for; matrix products, arithmetic and copies ran while one was open for 4% of the time, Pallas kernels for 0%

commit v1 on v0

v1 whole, which is shorter than its diff:
```python
import functools

import jax
import jax.numpy as jnp
from jax import lax
from jax.experimental import pallas as pl
from jax.experimental.pallas import tpu as pltpu
from jax.sharding import PartitionSpec as P

TILE = 64
LANES = 128


def partial_kernel(
    n_row, live_ref, vals_ref, rows_ref, cols_ref, src_ref, out_ref, pick, dense, swapped
):
    tiles_in, slots = pick.shape
    lanes = vals_ref.shape[-1]
    col_tiles = src_ref.shape[0] // TILE
    row_tiles = tiles_in // col_tiles
    half = tiles_in // 2
    chunk = min(half, 512)
    pairs = chunk // row_tiles

    @pl.when(pl.program_id(0) == 0)
    def _():
        row = rows_ref[0]
        col = cols_ref[0]
        slot = lax.broadcasted_iota(jnp.int32, (1, slots), 1)
        place = (col & 1) * half + (col >> 1) * row_tiles + row
        place = jnp.where(slot < live_ref[0, 0], place, -1)

        @pl.loop(0, tiles_in // 128)
        def _(at):
            first = pl.multiple_of(at * 128, 128)
            index = first + lax.broadcasted_iota(jnp.int32, (128, slots), 0)
            pick[pl.ds(first, 128), :] = jnp.where(index == place, 1.0, 0.0).astype(
                jnp.bfloat16
            )

        for pair in range(col_tiles // 2):
            low = 2 * pair * TILE
            swapped[low : low + TILE, :] = src_ref[low + TILE : low + 2 * TILE, :]
            swapped[low + TILE : low + 2 * TILE, :] = src_ref[low : low + TILE, :]

    is_low = lax.broadcasted_iota(jnp.int32, (row_tiles, LANES), 1) < TILE

    def one_chunk(at, carry):
        first = pl.multiple_of(at * chunk, chunk)
        for sub in range(lanes // 256):
            vals = vals_ref[0, 0, :, sub * 256 : (sub + 1) * 256]
            even = jnp.dot(
                pick[pl.ds(first, chunk), :], vals, preferred_element_type=jnp.float32
            )
            odd = jnp.dot(
                pick[pl.ds(half + first, chunk), :],
                vals,
                preferred_element_type=jnp.float32,
            )
            for part in range(2):
                block = 2 * sub + part
                for pair in range(pairs):
                    held = even[
                        pair * row_tiles : (pair + 1) * row_tiles,
                        part * LANES : (part + 1) * LANES,
                    ]
                    turned = pltpu.roll(
                        odd[
                            pair * row_tiles : (pair + 1) * row_tiles,
                            part * LANES : (part + 1) * LANES,
                        ],
                        TILE,
                        1,
                    )
                    lane = pl.multiple_of((at * pairs + pair) * LANES, LANES)
                    where = pl.ds(block * row_tiles, row_tiles), pl.ds(lane, LANES)
                    dense[(0,) + where] = jnp.where(is_low, held, turned).astype(
                        jnp.bfloat16
                    )
                    dense[(1,) + where] = jnp.where(is_low, turned, held).astype(
                        jnp.bfloat16
                    )
        return carry

    if half == chunk:
        one_chunk(0, 0)
    else:
        lax.fori_loop(0, half // chunk, one_chunk, 0)

    own = row_tiles // n_row
    for parity, source in ((0, src_ref), (1, swapped)):
        sums = jnp.dot(
            dense[parity], source[...], preferred_element_type=jnp.float32
        )
        for block in range(lanes // LANES):
            for owner in range(n_row):
                low = block * row_tiles + owner * own
                out_ref[owner, 2 * block + parity] = sums[low : low + own, :]


def partial_sums(n_row, live, vals, rows, cols, source):
    slots = vals.shape[2]
    width = source.shape[1]
    row_tiles = n_row * 8
    col_tiles = source.shape[0] // TILE
    tiles_in = row_tiles * col_tiles
    lanes = 1024
    blocks = lanes // LANES
    return pl.pallas_call(
        functools.partial(partial_kernel, n_row),
        grid=(vals.shape[3] // lanes,),
        in_specs=[
            pl.BlockSpec(memory_space=pltpu.SMEM),
            pl.BlockSpec((1, 1, slots, lanes), lambda k: (0, 0, 0, k)),
            pl.BlockSpec((1, 1, slots), lambda k: (0, 0, 0)),
            pl.BlockSpec((1, 1, slots), lambda k: (0, 0, 0)),
            pl.BlockSpec(source.shape, lambda k: (0, 0)),
        ],
        out_specs=pl.BlockSpec((n_row, 2 * blocks, 8, width), lambda k: (0, k, 0, 0)),
        out_shape=jax.ShapeDtypeStruct((n_row, TILE, 8, width), jnp.float32),
        scratch_shapes=[
            pltpu.VMEM((tiles_in, slots), jnp.bfloat16),
            pltpu.VMEM((2, blocks * row_tiles, source.shape[0] ), jnp.bfloat16),
            pltpu.VMEM(source.shape, jnp.bfloat16),
        ],
        compiler_params=pltpu.CompilerParams(vmem_limit_bytes=60 * 1024 * 1024),
    )(live, vals, rows, cols, source)


def on_device(features, tile_values, tile_rows, tile_cols, counts, weight, bias):
    piece_rows = features.shape[1]
    feat_width = features.shape[2]
    n_row = lax.axis_size("row")
    gathered = lax.all_gather(features, "col", axis=1, tiled=True)
    source = gathered.reshape(-1, feat_width)
    sums = partial_sums(n_row, counts, tile_values, tile_rows, tile_cols, source)
    own_rows = lax.psum_scatter(sums, "row", scatter_dimension=0, tiled=True)
    hidden = own_rows[0].astype(jnp.bfloat16).transpose(1, 0, 2).reshape(-1, feat_width)
    mixed = jnp.dot(hidden, weight, preferred_element_type=jnp.float32) + bias
    return jnp.maximum(mixed, 0.0).astype(jnp.bfloat16).reshape(1, piece_rows, feat_width)


def solution(mesh):
    in_specs = (
        P(("groups", "row"), "col", None),
        P(("groups", "row"), "col", None, None),
        P(("groups", "row"), "col", None),
        P(("groups", "row"), "col", None),
        P(("groups", "row"), "col"),
        P(),
        P(),
    )
    out_specs = P(("groups", "col"), "row", None)
    return jax.shard_map(
        on_device, mesh=mesh, in_specs=in_specs, out_specs=out_specs, check_vma=False
    )
```

time: 325 us -> 97.2 us (0.30)
  local copies, waits for them, and re-layouts: 170 us -> 0.06 us
  matrix products: 74.5 us -> 0.94 us
  Pallas kernels: 0 us -> 15.6 us
  waiting for transfers between devices: 53.8 us -> 65.2 us
  other arithmetic: 11.4 us -> 1.07 us
    while x40 -> x0, local copies, waits for them, and re-layouts: 88.5 us -> none
    dot_general x16 -> x0, matrix products: 72.6 us -> none  [the longest x8 45.2 us: block_step(): jnp.dot(selector, flat_products, precision=lax.Precision.HIGHEST, preferr...]
    dynamic_slice x16 -> x0, local copies, waits for them, and re-layouts: 34.2 us -> none  [block_step(): tile_block = lax.dynamic_slice_in_dim(values, first_slot, block_size, 0)]
    gather x8 -> x0, local copies, waits for them, and re-layouts: 32.1 us -> none  [block_step(): inputs = source[source_cols]]
    pallas_call x0 -> x1, Pallas kernels: none -> 15.6 us  [partial_sums(): pl.pallas_call(functools.partial(partial_kernel, n_row), grid=(vals.shape...]
    unnamed x5 -> x4, local copies, waits for them, and re-layouts: 12 us -> 0.01 us
    all_gather x1, waiting for transfers between devices: 9.02 us -> 20.4 us  [on_device(): gathered = lax.all_gather(features, 'col', axis=1, tiled=True)]
    select_n x8 -> x0, other arithmetic: 11.4 us -> none  [block_step(): inputs = source[source_cols]]
  transfers between devices with their start and end apart: 2 -> 2, of which waited for: 2 -> 2; matrix products, arithmetic and copies ran while one was open for 4% -> 0% of each run, Pallas kernels for 0% -> 0%
where the time goes in v1:
time: 97.2 us; the launch traced here: 97 us
  waiting for transfers between devices  65.2 us (67%)
  Pallas kernels  15.6 us (16%)
  between operations  14.1 us (15%)
  other arithmetic  1.07 us (1%)
    reduce_scatter x1, waiting for transfers between devices, on_device(): own_rows = lax.psum_scatter(sums, 'row', scatter_dimension=0, tiled=True)  44 us
    all_gather x1, waiting for transfers between devices, on_device(): gathered = lax.all_gather(features, 'col', axis=1, tiled=True)  20.4 us
    pallas_call x1, Pallas kernels, partial_sums(): pl.pallas_call(functools.partial(partial_kernel, n_row), grid=(vals.shape...  15.6 us
  transfers between devices with their start and end apart: 2, of which 2 were waited for; matrix products, arithmetic and copies ran while one was open for 0% of the time, Pallas kernels for 0%

profile of v1, /device:TPU:0, one launch (start us, length us, event | category | flops | bytes accessed | tf_op | source)
XLA Modules:
  0.0 97.0 jit_solution(3807492556676464520)
XLA Ops:
  6.5 0.0 copy-start
  6.5 0.0 copy-start.1
  6.5 0.0 all-gather.2.cloned.1.call-start
  6.5 0.7 all-gather.2.cloned.1.call-update
  7.3 0.0 reduce-scatter.2.cloned.1.call-start
  8.0 20.4 %all-gather.2.cloned.1.call-done = bf16[1,2048,256]{2,1,0:T(8,128)(2,1)} async-done(((bf16[1,512,256]{2,1,0:T(8,128)(2,1)}), bf16[1,2048,256]{2,1,0:T(8,128)(2,1)}) %all-gather.2.cloned.1.call-update) | async-done | bytes 1048592 | tf_op jit(solution)/shard_map/all_gather | solution.py:134
  28.4 15.6 %shard_map.73 = f32[4,64,8,256]{3,2,1,0:T(8,128)} custom-call(s32[1,1]{1,0:T(1,128)S(6)} %copy.9.live_ref, bf16[1,1,1024,4096]{3,2,1,0:T(8,128)(2,1)} %vals_ref.1, s32[1,1,1024]{2,1,0:T(1,128)} %rows_ref.1, s32[1,1,1024]{2,1,0:T(1,128)} %cols_ref.1, bf16[2048,256]{1,0:T(8,128)(2,1)} %bitcast.10), custom_call_target="tpu_custom_call" | custom-call | tf_op jit(solution)/shard_map/pallas_call | solution.py:109
  44.0 0.0 reduce-scatter.2.cloned.1.call-update
  44.0 44.0 %reduce-scatter.2.cloned.1.call-done = f32[1,64,8,256]{3,2,1,0:T(8,128)} async-done(((f32[4,64,8,256]{3,2,1,0:T(8,128)}), f32[1,64,8,256]{3,2,1,0:T(8,128)}) %reduce-scatter.2.cloned.1.call-update) | async-done | bytes 524304 | tf_op jit(solution)/shard_map/reduce_scatter | solution.py:137
  88.1 1.1 %convert_bitcast_fusion = bf16[8,64,256]{2,0,1:T(8,128)(2,1)S(1)} fusion(f32[1,64,8,256]{3,2,1,0:T(8,128)} %reduce-scatter.2.cloned.1.call-done), kind=kLoop, calls=%fused_computation.4 | loop fusion | flops 131072 | bytes 786432 | tf_op jit(solution)/shard_map/transpose | solution.py:138
  89.2 0.0 copy-done
  89.2 0.0 copy-done.1
  89.2 0.9 fusion.2
  (1 shorter events, 0.0 us)
Async XLA Ops:
  6.5 82.7 %copy-start = (bf16[256,256]{1,0:T(8,128)(2,1)S(1)}, bf16[256,256]{1,0:T(8,128)(2,1)}, u32[]{:S(2)}) copy-start(bf16[256,256]{1,0:T(8,128)(2,1)} %param.12) | copy-start | bytes 393220
  6.5 82.7 %copy-start.1 = (f32[256]{0:T(256)S(1)}, f32[256]{0:T(256)}, u32[]{:S(2)}) copy-start(f32[256]{0:T(256)} %param.13) | copy-start | bytes 3076
  6.5 21.8 %all-gather.2.cloned.1.call-start = ((), (), s32[]{:S(2)}) async-start(), calls=%async_computation.1 | async-start | bytes 1310720 | tf_op jit(solution)/shard_map/all_gather | solution.py:134
  7.3 80.8 %reduce-scatter.2.cloned.1.call-start = ((), (), s32[]{:S(2)}) async-start(), calls=%async_computation.2 | async-start | bytes 2621440 | tf_op jit(solution)/shard_map/reduce_scatter | solution.py:137
Sparse Core Ops, SparseCore 0:
  8.9 19.4 all-gather.1
  44.2 43.8 reduce-scatter.1

commit v2 on v0

v2 whole, which is shorter than its diff:
```python
import functools

import jax
import jax.numpy as jnp
from jax import lax
from jax.experimental import pallas as pl
from jax.experimental.pallas import tpu as pltpu
from jax.sharding import PartitionSpec as P

TILE = 64
LANES = 128
MESH = pl.DeviceIdType.MESH


def layer_kernel(
    n_row, n_col, live_ref, vals_hbm, rows_ref, cols_ref, feat_ref, weight_ref, bias_ref,
    out_ref, vals, pick, dense, src, swapped, acc, sent, up_in, down_in,
    vals_sem, far_send, far_recv, near_send, near_recv, send_sem, up_sem, down_sem,
):
    steps, slots, lanes = vals.shape
    tiles_in = pick.shape[0]
    piece_rows = feat_ref.shape[1]
    col_tiles = src.shape[0] // TILE
    row_tiles = tiles_in // col_tiles
    half = tiles_in // 2
    chunk = min(half, 512)
    pairs = chunk // row_tiles
    own = row_tiles // n_row
    blocks = lanes // LANES
    chips = n_col // 2
    z = lax.axis_index("row")
    me = lax.axis_index("col")
    core = lax.rem(me, 2)
    sibling = me + 1 - 2 * core

    def load(step):
        return pltpu.make_async_copy(
            vals_hbm.at[0, 0, :, pl.ds(pl.multiple_of(step * lanes, lanes), lanes)],
            vals.at[step], vals_sem.at[step],
        )

    for step in range(steps):
        load(step).start()

    def rows_of(index):
        return src.at[pl.ds(pl.multiple_of(index * piece_rows, piece_rows), piece_rows)]

    def far(d):
        return pltpu.make_async_remote_copy(
            src_ref=feat_ref.at[0], dst_ref=rows_of(me),
            send_sem=far_send.at[d], recv_sem=far_recv.at[d],
            device_id={"col": lax.rem(me + 2 * d, n_col)}, device_id_type=MESH,
        )

    def near(d):
        origin = lax.rem(me + n_col - 2 * d, n_col)
        return pltpu.make_async_remote_copy(
            src_ref=feat_ref.at[0] if d == 0 else rows_of(origin), dst_ref=rows_of(origin),
            send_sem=near_send.at[d], recv_sem=near_recv.at[d],
            device_id={"col": sibling}, device_id_type=MESH,
        )

    def passed(p, o, to, sem):
        landing = up_in if sem is up_sem else down_in
        return pltpu.make_async_remote_copy(
            src_ref=sent.at[p, o], dst_ref=landing.at[p, o],
            send_sem=send_sem.at[p, o], recv_sem=sem.at[p, o],
            device_id={"row": to}, device_id_type=MESH,
        )

    barrier = pltpu.get_barrier_semaphore()
    for d in range(1, chips):
        pl.semaphore_signal(
            barrier, inc=1, device_id={"col": lax.rem(me + 2 * d, n_col)}, device_id_type=MESH
        )
    pl.semaphore_signal(barrier, inc=1, device_id={"col": sibling}, device_id_type=MESH)

    @pl.when(z > 0)
    def _():
        pl.semaphore_signal(barrier, inc=1, device_id={"row": z - 1}, device_id_type=MESH)

    @pl.when(z < n_row - 1)
    def _():
        pl.semaphore_signal(barrier, inc=1, device_id={"row": z + 1}, device_id_type=MESH)

    beside = lax.div(z + n_row - 1, n_row) + lax.div(2 * n_row - 2 - z, n_row)
    pl.semaphore_wait(barrier, chips + beside)

    for d in range(1, chips):
        far(d).start()
    near(0).start()
    rows_of(me)[...] = feat_ref[0]

    slot = lax.broadcasted_iota(jnp.int32, (1, slots), 1)
    place = (cols_ref[0] & 1) * half + (cols_ref[0] >> 1) * row_tiles + rows_ref[0]
    place = jnp.where(slot < live_ref[0, 0], place, -1)

    @pl.loop(0, tiles_in // 128)
    def _(at):
        first = pl.multiple_of(at * 128, 128)
        index = first + lax.broadcasted_iota(jnp.int32, (128, slots), 0)
        pick[pl.ds(first, 128), :] = jnp.where(index == place, 1.0, 0.0).astype(jnp.bfloat16)

    is_low = lax.broadcasted_iota(jnp.int32, (row_tiles, LANES), 1) < TILE

    def densify(step):
        def one_chunk(at, carry):
            first = pl.multiple_of(at * chunk, chunk)
            for sub in range(lanes // 256):
                block_vals = vals[step, :, sub * 256 : (sub + 1) * 256]
                even = jnp.dot(
                    pick[pl.ds(first, chunk), :], block_vals,
                    preferred_element_type=jnp.float32,
                )
                odd = jnp.dot(
                    pick[pl.ds(half + first, chunk), :], block_vals,
                    preferred_element_type=jnp.float32,
                )
                for part in range(2):
                    block = 2 * sub + part
                    cut = slice(part * LANES, (part + 1) * LANES)
                    for pair in range(pairs):
                        down = slice(pair * row_tiles, (pair + 1) * row_tiles)
                        held = even[down, cut]
                        turned = pltpu.roll(odd[down, cut], TILE, 1)
                        lane = pl.multiple_of((at * pairs + pair) * LANES, LANES)
                        where = pl.ds(block * row_tiles, row_tiles), pl.ds(lane, LANES)
                        dense[(0,) + where] = jnp.where(is_low, held, turned).astype(jnp.bfloat16)
                        dense[(1,) + where] = jnp.where(is_low, turned, held).astype(jnp.bfloat16)
            return carry

        if half == chunk:
            one_chunk(0, 0)
        else:
            lax.fori_loop(0, half // chunk, one_chunk, 0)

    def finish_gather():
        for d in range(1, chips):
            far(d).wait_recv()
            near(d).start()
        for d in range(chips):
            near(d).wait_recv()
        for pair in range(col_tiles // 2):
            low = 2 * pair * TILE
            swapped[low : low + TILE, :] = src[low + TILE : low + 2 * TILE, :]
            swapped[low + TILE : low + 2 * TILE, :] = src[low : low + TILE, :]

    def multiply(step):
        for parity, source in ((0, src), (1, swapped)):
            sums = jnp.dot(dense[parity], source[...], preferred_element_type=jnp.float32)
            for block in range(blocks):
                for owner in range(n_row):
                    low = block * row_tiles + owner * own
                    to = (2 * block + parity) * own
                    acc[step, owner, to : to + own, :] = sums[low : low + own, :]

    def pass_on(p, is_first, sem, landing, to, owner_of, count):
        def one(j, carry):
            o = owner_of(j)

            @pl.when(is_first)
            def _():
                sent[p, o] = acc[p, o].astype(jnp.bfloat16)

            @pl.when(jnp.logical_not(is_first))
            def _():
                passed(p, o, to, sem).wait_recv()
                sent[p, o] = (acc[p, o] + landing[p, o].astype(jnp.float32)).astype(jnp.bfloat16)

            passed(p, o, to, sem).start()
            return carry

        lax.fori_loop(0, count, one, 0)

        @pl.when(jnp.logical_not(is_first))
        def _():
            passed(p, z, to, sem).wait_recv()
            acc[p, z] = acc[p, z] + landing[p, z].astype(jnp.float32)

    def one_step(t, carry):
        @pl.when(t < steps)
        def _():
            load(t).wait()
            densify(t)

            @pl.when(t == 0)
            def _():
                finish_gather()

            multiply(t)

        up = t - z

        @pl.when(jnp.logical_and(up >= 0, up < steps))
        def _():
            pass_on(up, z == 0, up_sem, up_in, z + 1, lambda j: n_row - 1 - j, n_row - 1 - z)

        below = t - (n_row - 1 - z)

        @pl.when(jnp.logical_and(below >= 0, below < steps))
        def _():
            pass_on(below, z == n_row - 1, down_sem, down_in, z - 1, lambda j: j, z)

        return carry

    lax.fori_loop(0, steps + n_row - 1, one_step, 0)

    hidden = jnp.concatenate([acc[p, z].astype(jnp.bfloat16) for p in range(steps)], axis=0)
    target = lax.broadcasted_iota(jnp.int32, (piece_rows, piece_rows), 0)
    origin = lax.broadcasted_iota(jnp.int32, (piece_rows, piece_rows), 1)
    wanted = (target & (TILE - 1)) * own + (target >> 6)
    order = jnp.where(origin == wanted, 1.0, 0.0).astype(jnp.bfloat16)
    hidden = jnp.dot(order, hidden, preferred_element_type=jnp.float32).astype(jnp.bfloat16)
    mixed = jnp.dot(hidden, weight_ref[...], preferred_element_type=jnp.float32) + bias_ref[...]
    out_ref[0] = jnp.maximum(mixed, 0.0).astype(jnp.bfloat16)

    for d in range(1, chips):
        far(d).wait_send()
    for d in range(chips):
        near(d).wait_send()

    def drain(p, carry):
        def up_one(o, inner):
            passed(p, o, z + 1, up_sem).wait_send()
            return inner

        def down_one(o, inner):
            passed(p, o, z - 1, down_sem).wait_send()
            return inner

        lax.fori_loop(z + 1, n_row, up_one, 0)
        lax.fori_loop(0, z, down_one, 0)
        return carry

    lax.fori_loop(0, steps, drain, 0)


def on_device(features, tile_values, tile_rows, tile_cols, counts, weight, bias):
    n_row, n_col = lax.axis_size("row"), lax.axis_size("col")
    piece_rows, width = features.shape[1:]
    slots, entries = tile_values.shape[2:]
    own = piece_rows // TILE
    row_tiles = n_row * own
    source_rows = n_col * piece_rows
    tiles_in = row_tiles * source_rows // TILE
    steps = 4 if tiles_in <= 2048 else 8
    lanes = entries // steps
    blocks = lanes // LANES
    part_rows = 2 * blocks * own
    vmem = pl.BlockSpec(memory_space=pltpu.VMEM)
    slabs = (steps, n_row, part_rows, width)
    dma = pltpu.SemaphoreType.DMA
    return pl.pallas_call(
        functools.partial(layer_kernel, n_row, n_col),
        in_specs=[
            pl.BlockSpec(memory_space=pltpu.SMEM), pl.BlockSpec(memory_space=pl.ANY),
            vmem, vmem, vmem, vmem, vmem,
        ],
        out_specs=vmem,
        out_shape=jax.ShapeDtypeStruct((1, piece_rows, width), jnp.bfloat16),
        scratch_shapes=[
            pltpu.VMEM((steps, slots, lanes), jnp.bfloat16),
            pltpu.VMEM((tiles_in, slots), jnp.bfloat16),
            pltpu.VMEM((2, blocks * row_tiles, source_rows), jnp.bfloat16),
            pltpu.VMEM((source_rows, width), jnp.bfloat16),
            pltpu.VMEM((source_rows, width), jnp.bfloat16),
            pltpu.VMEM(slabs, jnp.float32),
            pltpu.VMEM(slabs, jnp.bfloat16),
            pltpu.VMEM(slabs, jnp.bfloat16),
            pltpu.VMEM(slabs, jnp.bfloat16),
            dma((steps,)), dma((n_col // 2,)), dma((n_col // 2,)),
            dma((n_col // 2,)), dma((n_col // 2,)),
            dma((steps, n_row)), dma((steps, n_row)), dma((steps, n_row)),
        ],
        compiler_params=pltpu.CompilerParams(
            collective_id=0, has_side_effects=True, vmem_limit_bytes=62 * 1024 * 1024
        ),
    )(counts, tile_values, tile_rows, tile_cols, features, weight, bias.reshape(1, width))


def solution(mesh):
    in_specs = (
        P(("groups", "row"), "col", None),
        P(("groups", "row"), "col", None, None),
        P(("groups", "row"), "col", None),
        P(("groups", "row"), "col", None),
        P(("groups", "row"), "col"),
        P(),
        P(),
    )
    out_specs = P(("groups", "col"), "row", None)
    return jax.shard_map(
        on_device, mesh=mesh, in_specs=in_specs, out_specs=out_specs, check_vma=False
    )
```

time: 325 us -> 43.1 us (0.13)
  local copies, waits for them, and re-layouts: 170 us -> 1.67 us
  matrix products: 74.5 us -> 0 us
  waiting for transfers between devices: 53.8 us -> 0 us
  Pallas kernels: 0 us -> 40.6 us
  between operations: 13.4 us -> 0.66 us
  other arithmetic: 11.4 us -> 0 us
    while x40 -> x0, local copies, waits for them, and re-layouts: 88.5 us -> none
    dot_general x17 -> x0, matrix products: 74.5 us -> none  [the longest x8 45.2 us: block_step(): jnp.dot(selector, flat_products, precision=lax.Precision.HIGHEST, preferr...]
    reduce_scatter x1 -> x0, waiting for transfers between devices: 44 us -> none  [on_device(): lax.psum_scatter(partial_value, 'row', scatter_dimension=0, tiled=True)]
    pallas_call x0 -> x1, Pallas kernels: none -> 40.6 us  [on_device(): pl.pallas_call(functools.partial(layer_kernel, n_row, n_col), in_specs=[p...]
    dynamic_slice x16 -> x0, local copies, waits for them, and re-layouts: 34.2 us -> none  [block_step(): tile_block = lax.dynamic_slice_in_dim(values, first_slot, block_size, 0)]
    gather x8 -> x0, local copies, waits for them, and re-layouts: 32.1 us -> none  [block_step(): inputs = source[source_cols]]
    select_n x8 -> x0, other arithmetic: 11.4 us -> none  [block_step(): inputs = source[source_cols]]
    unnamed x5 -> x1, local copies, waits for them, and re-layouts: 12 us -> 1.67 us
  transfers between devices with their start and end apart: 2 -> 0, of which waited for: 2 -> 0; matrix products, arithmetic and copies ran while one was open for 4% -> 0% of each run, Pallas kernels for 0% -> 0%
where the time goes in v2:
time: 43.1 us; the launch traced here: 42.9 us
  Pallas kernels  40.6 us (94%)
  local copies, waits for them, and re-layouts  1.67 us (4%)
  between operations  0.66 us (2%)
    pallas_call x1, Pallas kernels, on_device(): pl.pallas_call(functools.partial(layer_kernel, n_row, n_col), in_specs=[p...  40.6 us
    unnamed x1, local copies, waits for them, and re-layouts  1.67 us

profile of v2, /device:TPU:0, one launch (start us, length us, event | category | flops | bytes accessed | tf_op | source)
XLA Modules:
  0.0 42.9 jit_solution(15554247551584009536)
XLA Ops:
  0.7 40.6 %shard_map.73 = bf16[1,512,256]{2,1,0:T(8,128)(2,1)} custom-call(s32[1,1]{1,0:T(1,128)S(6)} %copy.9.live_ref, bf16[1,1,1024,4096]{3,2,1,0:T(8,128)(2,1)} %vals_hbm.1, s32[1,1,1024]{2,1,0:T(1,128)} %rows_ref.1, s32[1,1,1024]{2,1,0:T(1,128)} %cols_ref.1, bf16[1,512,256]{2,1,0:T(8,128)(2,1)} %feat_ref.1, bf16[256,256]{1,0:T(8,128)(2,1)} %weight_ref.1, ...), custom_call_target="tpu_custom_call" | custom-call | tf_op jit(solution)/shard_map/pallas_call | solution.py:253
  41.2 1.7 %copy.10 = bf16[1,512,256]{2,1,0:T(8,128)(2,1)} copy(bf16[1,512,256]{2,1,0:T(8,128)(2,1)} %shard_map.73) | data formatting | bytes 524288

commit v3 on v2

--- a/solution.py
+++ b/solution.py
@@ -154,7 +154,7 @@
                     to = (2 * block + parity) * own
                     acc[step, owner, to : to + own, :] = sums[low : low + own, :]
 
-    def pass_on(p, is_first, sem, landing, to, owner_of, count):
+    def pass_on(p, is_first, sem, landing, to, owner_of, begin, end):
         def one(j, carry):
             o = owner_of(j)
 
@@ -170,12 +170,18 @@
             passed(p, o, to, sem).start()
             return carry
 
-        lax.fori_loop(0, count, one, 0)
-
-        @pl.when(jnp.logical_not(is_first))
-        def _():
-            passed(p, z, to, sem).wait_recv()
-            acc[p, z] = acc[p, z] + landing[p, z].astype(jnp.float32)
+        lax.fori_loop(begin, end, one, 0)
+
+    above_count = n_row - 1 - z
+    below_count = z
+    above_early = jnp.minimum(above_count, jnp.maximum(above_count - 1, 1))
+    below_early = jnp.minimum(below_count, jnp.maximum(below_count - 1, 1))
+
+    def pass_up(p, begin, end):
+        pass_on(p, z == 0, up_sem, up_in, z + 1, lambda j: n_row - 1 - j, begin, end)
+
+    def pass_down(p, begin, end):
+        pass_on(p, z == n_row - 1, down_sem, down_in, z - 1, lambda j: j, begin, end)
 
     def one_step(t, carry):
         @pl.when(t < steps)
@@ -193,17 +199,39 @@
 
         @pl.when(jnp.logical_and(up >= 0, up < steps))
         def _():
-            pass_on(up, z == 0, up_sem, up_in, z + 1, lambda j: n_row - 1 - j, n_row - 1 - z)
+            pass_up(up, 0, above_early)
 
         below = t - (n_row - 1 - z)
 
         @pl.when(jnp.logical_and(below >= 0, below < steps))
         def _():
-            pass_on(below, z == n_row - 1, down_sem, down_in, z - 1, lambda j: j, z)
+            pass_down(below, 0, below_early)
 
         return carry
 
     lax.fori_loop(0, steps + n_row - 1, one_step, 0)
+
+    def late(p, carry):
+        pass_up(p, above_early, above_count)
+        pass_down(p, below_early, below_count)
+        return carry
+
+    lax.fori_loop(0, steps, late, 0)
+
+    def collect(p, carry):
+        @pl.when(z > 0)
+        def _():
+            passed(p, z, z + 1, up_sem).wait_recv()
+            acc[p, z] = acc[p, z] + up_in[p, z].astype(jnp.float32)
+
+        @pl.when(z < n_row - 1)
+        def _():
+            passed(p, z, z - 1, down_sem).wait_recv()
+            acc[p, z] = acc[p, z] + down_in[p, z].astype(jnp.float32)
+
+        return carry
+
+    lax.fori_loop(0, steps, collect, 0)
 
     hidden = jnp.concatenate([acc[p, z].astype(jnp.bfloat16) for p in range(steps)], axis=0)
     target = lax.broadcasted_iota(jnp.int32, (piece_rows, piece_rows), 0)

time: 43.1 us -> 40.6 us (0.942)
  the two profiles are of different devices: /device:TPU:0 before, /device:TPU:19 now
where the time goes in v3:
time: 40.6 us; the launch traced here: 40.4 us
  Pallas kernels  38.1 us (94%)
  local copies, waits for them, and re-layouts  1.67 us (4%)
  between operations  0.66 us (2%)
    pallas_call x1, Pallas kernels, on_device(): pl.pallas_call(functools.partial(layer_kernel, n_row, n_col), in_specs=[p...  38.1 us
    unnamed x1, local copies, waits for them, and re-layouts  1.67 us

profile of v3, /device:TPU:19, one launch (start us, length us, event | category | flops | bytes accessed | tf_op | source)
XLA Modules:
  0.0 40.4 jit_solution(6978295111260820399)
XLA Ops:
  0.7 38.1 %shard_map.73 = bf16[1,512,256]{2,1,0:T(8,128)(2,1)} custom-call(s32[1,1]{1,0:T(1,128)S(6)} %copy.9.live_ref, bf16[1,1,1024,4096]{3,2,1,0:T(8,128)(2,1)} %vals_hbm.1, s32[1,1,1024]{2,1,0:T(1,128)} %rows_ref.1, s32[1,1,1024]{2,1,0:T(1,128)} %cols_ref.1, bf16[1,512,256]{2,1,0:T(8,128)(2,1)} %feat_ref.1, bf16[256,256]{1,0:T(8,128)(2,1)} %weight_ref.1, ...), custom_call_target="tpu_custom_call" | custom-call | tf_op jit(solution)/shard_map/pallas_call | solution.py:281
  38.7 1.7 %copy.10 = bf16[1,512,256]{2,1,0:T(8,128)(2,1)} copy(bf16[1,512,256]{2,1,0:T(8,128)(2,1)} %shard_map.73) | data formatting | bytes 524288

commit v4 on v3

--- a/solution.py
+++ b/solution.py
@@ -18,6 +18,7 @@
     vals_sem, far_send, far_recv, near_send, near_recv, send_sem, up_sem, down_sem,
 ):
     steps, slots, lanes = vals.shape
+    cuts = far_send.shape[1]
     tiles_in = pick.shape[0]
     piece_rows = feat_ref.shape[1]
     col_tiles = src.shape[0] // TILE
@@ -42,21 +43,25 @@
     for step in range(steps):
         load(step).start()
 
-    def rows_of(index):
-        return src.at[pl.ds(pl.multiple_of(index * piece_rows, piece_rows), piece_rows)]
-
-    def far(d):
+    cut_rows = piece_rows // cuts
+
+    def rows_of(index, cut):
+        first = pl.multiple_of(index * piece_rows + cut * cut_rows, cut_rows)
+        return src.at[pl.ds(first, cut_rows)]
+
+    def far(d, cut):
         return pltpu.make_async_remote_copy(
-            src_ref=feat_ref.at[0], dst_ref=rows_of(me),
-            send_sem=far_send.at[d], recv_sem=far_recv.at[d],
+            src_ref=feat_ref.at[0, pl.ds(cut * cut_rows, cut_rows)], dst_ref=rows_of(me, cut),
+            send_sem=far_send.at[d, cut], recv_sem=far_recv.at[d, cut],
             device_id={"col": lax.rem(me + 2 * d, n_col)}, device_id_type=MESH,
         )
 
-    def near(d):
+    def near(d, cut):
         origin = lax.rem(me + n_col - 2 * d, n_col)
+        mine = feat_ref.at[0, pl.ds(cut * cut_rows, cut_rows)]
         return pltpu.make_async_remote_copy(
-            src_ref=feat_ref.at[0] if d == 0 else rows_of(origin), dst_ref=rows_of(origin),
-            send_sem=near_send.at[d], recv_sem=near_recv.at[d],
+            src_ref=mine if d == 0 else rows_of(origin, cut), dst_ref=rows_of(origin, cut),
+            send_sem=near_send.at[d, cut], recv_sem=near_recv.at[d, cut],
             device_id={"col": sibling}, device_id_type=MESH,
         )
 
@@ -87,9 +92,11 @@
     pl.semaphore_wait(barrier, chips + beside)
 
     for d in range(1, chips):
-        far(d).start()
-    near(0).start()
-    rows_of(me)[...] = feat_ref[0]
+        for cut in range(cuts):
+            far(d, cut).start()
+    for cut in range(cuts):
+        near(0, cut).start()
+    src[pl.ds(pl.multiple_of(me * piece_rows, piece_rows), piece_rows), :] = feat_ref[0]
 
     slot = lax.broadcasted_iota(jnp.int32, (1, slots), 1)
     place = (cols_ref[0] & 1) * half + (cols_ref[0] >> 1) * row_tiles + rows_ref[0]
@@ -136,10 +143,12 @@
 
     def finish_gather():
         for d in range(1, chips):
-            far(d).wait_recv()
-            near(d).start()
+            for cut in range(cuts):
+                far(d, cut).wait_recv()
+                near(d, cut).start()
         for d in range(chips):
-            near(d).wait_recv()
+            for cut in range(cuts):
+                near(d, cut).wait_recv()
         for pair in range(col_tiles // 2):
             low = 2 * pair * TILE
             swapped[low : low + TILE, :] = src[low + TILE : low + 2 * TILE, :]
@@ -243,9 +252,11 @@
     out_ref[0] = jnp.maximum(mixed, 0.0).astype(jnp.bfloat16)
 
     for d in range(1, chips):
-        far(d).wait_send()
+        for cut in range(cuts):
+            far(d, cut).wait_send()
     for d in range(chips):
-        near(d).wait_send()
+        for cut in range(cuts):
+            near(d, cut).wait_send()
 
     def drain(p, carry):
         def up_one(o, inner):
@@ -271,7 +282,7 @@
     row_tiles = n_row * own
     source_rows = n_col * piece_rows
     tiles_in = row_tiles * source_rows // TILE
-    steps = 4 if tiles_in <= 2048 else 8
+    steps = 2 if tiles_in <= 2048 else 8
     lanes = entries // steps
     blocks = lanes // LANES
     part_rows = 2 * blocks * own
@@ -296,8 +307,8 @@
             pltpu.VMEM(slabs, jnp.bfloat16),
             pltpu.VMEM(slabs, jnp.bfloat16),
             pltpu.VMEM(slabs, jnp.bfloat16),
-            dma((steps,)), dma((n_col // 2,)), dma((n_col // 2,)),
-            dma((n_col // 2,)), dma((n_col // 2,)),
+            dma((steps,)), dma((n_col // 2, 4)), dma((n_col // 2, 4)),
+            dma((n_col // 2, 4)), dma((n_col // 2, 4)),
             dma((steps, n_row)), dma((steps, n_row)), dma((steps, n_row)),
         ],
         compiler_params=pltpu.CompilerParams(

time: 40.6 us -> 40.2 us (level)
  the two profiles are of different devices: /device:TPU:19 before, /device:TPU:0 now
where the time goes in v4:
time: 40.2 us; the launch traced here: 39.7 us
  Pallas kernels  37.4 us (93%)
  local copies, waits for them, and re-layouts  1.67 us (4%)
  between operations  0.66 us (2%)
    pallas_call x1, Pallas kernels, on_device(): pl.pallas_call(functools.partial(layer_kernel, n_row, n_col), in_specs=[p...  37.4 us
    unnamed x1, local copies, waits for them, and re-layouts  1.67 us

profile of v4, /device:TPU:0, one launch (start us, length us, event | category | flops | bytes accessed | tf_op | source)
XLA Modules:
  0.0 39.7 jit_solution(15061713892548867755)
XLA Ops:
  0.7 37.4 %shard_map.73 = bf16[1,512,256]{2,1,0:T(8,128)(2,1)} custom-call(s32[1,1]{1,0:T(1,128)S(6)} %copy.9.live_ref, bf16[1,1,1024,4096]{3,2,1,0:T(8,128)(2,1)} %vals_hbm.1, s32[1,1,1024]{2,1,0:T(1,128)} %rows_ref.1, s32[1,1,1024]{2,1,0:T(1,128)} %cols_ref.1, bf16[1,512,256]{2,1,0:T(8,128)(2,1)} %feat_ref.1, bf16[256,256]{1,0:T(8,128)(2,1)} %weight_ref.1, ...), custom_call_target="tpu_custom_call" | custom-call | tf_op jit(solution)/shard_map/pallas_call | solution.py:292
  38.0 1.7 %copy.10 = bf16[1,512,256]{2,1,0:T(8,128)(2,1)} copy(bf16[1,512,256]{2,1,0:T(8,128)(2,1)} %shard_map.73) | data formatting | bytes 524288
